TPU v7x, 768 devices: a whole 4x8x12 slice. The times are simulated.
768 devices in a mesh: dom: 96 (over y, x, z_hi), ens: 8 (over z_lo, core).
Axes of the slice: x: 4, y: 8, z: 12 (z_hi: 3, z_lo: 4; z = z_hi * 4 + z_lo), core: 2. Of those that a mesh axis runs over, the one named last changes fastest.
Arguments:
- members: bfloat16 [16, 2, 120, 196608], P('ens', None, None, 'dom'), may hold values from -6 to 6
- increment: bfloat16 [2, 120, 196608], P(None, None, 'dom'), may hold values from -6 to 6
- vert_loc: float32 [120, 120], replicated, may hold values from -0.5 to 0.5
- tiles: bfloat16 [48, 4, 128, 128], replicated, may hold values from -0.25 to 0.25
- tile_cols: int32 [48, 4], replicated, may hold values from 0 to 47, as said below
- coarse_of: int32 [196608], P('dom'), may hold values from 0 to 63
Outputs:
- covaried: bfloat16 [2, 120, 196608], P(None, None, ('dom', 'ens'))
Inputs may be any that keep to these rules, and one draw needn't show every extreme that they name: `tile_cols`: each row lists 4 different blocks; the first is the row's own block.
All inputs are finite; a program needn't handle non-finite values.
Results may differ from a plain program's by a relative error of at most 0.0049.
Values may be sent and summed in bfloat16 or wider, within the bound.
A program may use at most 32 MiB of HBM per device.

v0:
```python
import jax
import jax.numpy as jnp
from jax import lax
from jax.sharding import PartitionSpec as P

NCO_DEV = 64


def shards(members, increment, vert_loc, tiles, tile_cols, coarse_of):
    highest = lax.Precision.HIGHEST
    mem_dev, nvars, nlev, col_dev = members.shape
    nblocks = tiles.shape[0]
    tile_len = tiles.shape[2]
    n_ens = lax.axis_size("ens")
    total_mem = mem_dev * n_ens
    onehot = (coarse_of[:, None] == jnp.arange(NCO_DEV, dtype=jnp.int32)[None, :]).astype(
        jnp.float32
    )
    weighted = members.astype(jnp.float32) * increment.astype(jnp.float32)[None]
    vertical = jnp.einsum("lm,kcmn->kcln", vert_loc, weighted, precision=highest)
    summed = jnp.einsum("kcln,np->kclp", vertical, onehot, precision=highest)
    coarse = summed.astype(jnp.bfloat16).reshape(mem_dev * nvars * nlev, NCO_DEV)
    slabs = lax.all_to_all(coarse, "dom", split_axis=0, concat_axis=1, tiled=True)
    share = slabs.shape[0]
    blocks = slabs.reshape(share, nblocks, tile_len)
    picked = blocks[:, tile_cols, :]
    smoothed = jnp.einsum("btij,sbtj->sbi", tiles, picked, preferred_element_type=jnp.float32)
    smoothed = smoothed.reshape(share, nblocks * tile_len)
    returned = lax.all_to_all(smoothed, "dom", split_axis=1, concat_axis=0, tiled=True)
    local_coarse = returned.reshape(mem_dev, nvars, nlev, NCO_DEV)
    spread = jnp.einsum("kclp,np->kcln", local_coarse, onehot, precision=highest)
    terms = jnp.sum(members.astype(jnp.float32) * spread, axis=0)
    total = lax.psum_scatter(terms, "ens", scatter_dimension=2, tiled=True)
    return (total / (total_mem - 1)).astype(jnp.bfloat16)


def solution(mesh):
    return jax.shard_map(
        shards,
        mesh=mesh,
        in_specs=(P("ens", None, None, "dom"), P(None, None, "dom"), P(), P(), P(), P("dom")),
        out_specs=P(None, None, ("dom", "ens")),
        check_vma=False,
    )
```

profile of v0, /device:TPU:1, one launch (start us, length us, event | category | flops | bytes accessed | tf_op | source)
XLA Modules:
  0.0 133.0 jit_solution(16664160102627828982)
XLA Ops:
  6.5 0.0 copy-start
  6.5 0.0 copy-start.1
  6.5 1.6 %convert_element_type.15 = f32[2,120,2048]{2,1,0:T(8,128)S(1)} convert(bf16[2,120,2048]{2,1,0:T(8,128)(2,1)} %param.7) | non-fusion elementwise | flops 491520 | bytes 2949120 | tf_op jit(solution)/shard_map/convert_element_type | solution.py:19
  8.1 0.0 copy-done
  8.1 0.3 copy-done.1
  8.4 0.0 copy-start.2
  8.4 5.3 %fusion = f32[2,2,2048,120]{2,3,1,0:T(8,128)S(1)} fusion(bf16[2,2,120,2048]{3,2,1,0:T(8,128)(2,1)S(1)} %copy-done.1, f32[2,120,2048]{2,1,0:T(8,128)S(1)} %convert_element_type.15, f32[120,120]{1,0:T(8,128)S(1)} %copy-done), kind=kOutput, calls=%fused_computation.3 | convolution fusion | flops 1417543680 | bytes 7921920 | tf_op jit(solution)/shard_map/lm,kcmn->kcln/dot_general | solution.py:20
  13.7 0.0 copy-done.2
  13.7 0.0 copy-start.3
  13.7 2.2 %fusion.5 = bf16[2,2,120,64]{2,3,1,0:T(8,128)(2,1)S(1)} fusion(f32[2,2,2048,120]{2,3,1,0:T(8,128)S(1)} %fusion, s32[2048]{0:T(1024)S(1)} %copy-done.2), kind=kOutput, calls=%fused_computation.9 | convolution fusion | flops 755136512 | bytes 4001792 | tf_op jit(solution)/shard_map/kcln,np->kclp/dot_general | solution.py:21
  15.9 0.1 copy.14
  16.0 0.1 all_to_all.24
  16.1 0.8 reshape.35
  16.9 23.8 %all-to-all-start = ((bf16[96,2,160]{2,1,0:T(2,128)(2,1)}), bf16[96,2,160]{2,1,0:T(2,128)(2,1)S(1)}, u32[]{:S(2)}, u32[]{:S(2)}) async-start(bf16[96,2,160]{2,1,0:T(2,128)(2,1)} %reshape.35), calls=%async_computation | async-start | bytes 196608 | tf_op jit(solution)/shard_map/all_to_all | solution.py:23
  40.7 0.0 reduce-scatter.2.cloned.1.call-start
  40.8 0.0 copy-done.3
  40.8 0.1 copy.16
  40.9 0.1 reshape.24
  41.0 13.2 %all-to-all-done = bf16[96,2,160]{2,1,0:T(2,128)(2,1)S(1)} async-done(((bf16[96,2,160]{2,1,0:T(2,128)(2,1)}), bf16[96,2,160]{2,1,0:T(2,128)(2,1)S(1)}, u32[]{:S(2)}, u32[]{:S(2)}) %all-to-all-start) | async-done | bytes 61472 | tf_op jit(solution)/shard_map/all_to_all | solution.py:23
  54.2 0.2 reshape.36
  54.4 0.1 reshape.20
  54.5 0.7 gather_fusion
  55.3 4.5 %convolution_bitcast_fusion = f32[5,48,128]{2,0,1:T(8,128)S(1)} fusion(bf16[5,48,4,128]{3,0,2,1:T(8,128)(2,1)S(1)} %bitcast.38, bf16[48,4,128,128]{3,2,1,0:T(8,128)(2,1)} %param.9), kind=kOutput, calls=%fused_computation.8 | convolution fusion | flops 31457280 | bytes 6660096 | tf_op jit(solution)/shard_map/btij,sbtj->sbi/dot_general | solution.py:27
  59.8 0.1 all_to_all.27
  59.9 0.2 copy.26
  60.1 0.2 reshape.37
  60.3 20.1 %all_to_all.32 = f32[96,1,320]{2,1,0:T(1,128)S(1)} all-to-all(f32[96,1,320]{2,1,0:T(1,128)S(1)} %reshape.37), channel_id=1, replica_groups=mesh['dom'=96,'ens'=8] {'dom'}, dimensions={0} | all-to-all | bytes 245760 | tf_op jit(solution)/shard_map/all_to_all | solution.py:29
  80.4 0.5 broadcast.7
  81.0 1.0 reduce
  82.0 0.1 reshape.38
  82.1 3.2 %fusion.1 = f32[2,120,2048]{2,1,0:T(8,128)} fusion(bf16[2,2,120,2048]{3,2,1,0:T(8,128)(2,1)S(1)} %copy-done.1, f32[2,2,120,64]{3,2,1,0:T(8,128)S(1)} %reshape.21, s32[2048]{0:T(1024)S(1)} %copy-done.2), kind=kOutput, calls=%fused_computation.4 | convolution fusion | flops 757563392 | bytes 4063232 | tf_op jit(solution)/shard_map/kclp,np->kcln/dot_general | solution.py:31
  85.4 0.0 reduce-scatter.2.cloned.1.call-update
  85.4 39.1 %reduce-scatter.2.cloned.1.call-done = f32[2,120,256]{2,1,0:T(8,128)} async-done(((f32[2,120,2048]{2,1,0:T(8,128)}), f32[2,120,256]{2,1,0:T(8,128)}) %reduce-scatter.2.cloned.1.call-update) | async-done | bytes 245776 | tf_op jit(solution)/shard_map/reduce_scatter | solution.py:33
  124.5 1.6 %multiply_convert_fusion = bf16[2,120,256]{2,1,0:T(8,128)(2,1)} fusion(f32[2,120,256]{2,1,0:T(8,128)} %reduce-scatter.2.cloned.1.call-done), kind=kLoop, calls=%fused_computation.14 | loop fusion | flops 122880 | bytes 368640 | tf_op jit(solution)/shard_map/convert_element_type | solution.py:34
  (7 shorter events, 0.2 us)
Async XLA Ops:
  6.5 1.6 %copy-start = (f32[120,120]{1,0:T(8,128)S(1)}, f32[120,120]{1,0:T(8,128)}, u32[]{:S(2)}) copy-start(f32[120,120]{1,0:T(8,128)} %param.8) | copy-start | bytes 172804
  6.5 1.9 %copy-start.1 = (bf16[2,2,120,2048]{3,2,1,0:T(8,128)(2,1)S(1)}, bf16[2,2,120,2048]{3,2,1,0:T(8,128)(2,1)}, u32[]{:S(2)}) copy-start(bf16[2,2,120,2048]{3,2,1,0:T(8,128)(2,1)} %param.6) | copy-start | bytes 5898244
  8.4 5.3 %copy-start.2 = (s32[2048]{0:T(1024)S(1)}, s32[2048]{0:T(1024)}, u32[]{:S(2)}) copy-start(s32[2048]{0:T(1024)} %param.11) | copy-start | bytes 24580
  13.7 27.1 %copy-start.3 = (s32[48,4]{0,1:T(4,128)S(1)}, s32[48,4]{0,1:T(4,128)}, u32[]{:S(2)}) copy-start(s32[48,4]{0,1:T(4,128)} %param.10) | copy-start | bytes 2308
  16.9 37.3 %all-to-all-start = ((bf16[96,2,160]{2,1,0:T(2,128)(2,1)}), bf16[96,2,160]{2,1,0:T(2,128)(2,1)S(1)}, u32[]{:S(2)}, u32[]{:S(2)}) async-start(bf16[96,2,160]{2,1,0:T(2,128)(2,1)} %reshape.35), calls=%async_computation | async-start | bytes 196608 | tf_op jit(solution)/shard_map/all_to_all | solution.py:23
  40.7 83.8 %reduce-scatter.2.cloned.1.call-start = ((), (), s32[]{:S(2)}) async-start(), calls=%async_computation.3 | async-start | bytes 2211840 | tf_op jit(solution)/shard_map/reduce_scatter | solution.py:33
Sparse Core Ops, SparseCore 0:
  85.5 38.9 reduce-scatter.1
where the time goes:
time: 135 us; the launch traced here: 133 us
  waiting for transfers between devices  52.3 us (39%)
  starting transfers between devices  23.8 us (18%)
  blocking collectives  20.1 us (15%)
  matrix products  15.2 us (11%)
  between operations  13.6 us (10%)
  other arithmetic  4.18 us (3%)
  local copies, waits for them, and re-layouts  3.71 us (3%)
    reduce_scatter x1, waiting for transfers between devices, shards(): total = lax.psum_scatter(terms, 'ens', scatter_dimension=2, tiled=True)  39.1 us
    all_to_all x1, starting transfers between devices, shards(): lax.all_to_all(coarse, 'dom', split_axis=0, concat_axis=1, tiled=True)  23.8 us
    all_to_all x1, blocking collectives, shards(): lax.all_to_all(smoothed, 'dom', split_axis=1, concat_axis=0, tiled=True)  20.1 us
    all_to_all x1, waiting for transfers between devices, shards(): lax.all_to_all(coarse, 'dom', split_axis=0, concat_axis=1, tiled=True)  13.2 us
    dot_general x1, matrix products, shards(): jnp.einsum('lm,kcmn->kcln', vert_loc, weighted, precision=highest)  5.26 us
    dot_general x1, matrix products, shards(): jnp.einsum('btij,sbtj->sbi', tiles, picked, preferred_element_type=jnp.fl...  4.51 us
    dot_general x1, matrix products, shards(): jnp.einsum('kclp,np->kcln', local_coarse, onehot, precision=highest)  3.21 us
  transfers between devices with their start and end apart: 2, of which 2 were waited for; matrix products, arithmetic and copies ran while one was open for 0% of the time, Pallas kernels for 0%

commit v1 on v0

v1 whole, which is shorter than its diff:
```python
import jax
import jax.numpy as jnp
from jax import lax
from jax.experimental import pallas as pl
from jax.experimental.pallas import tpu as pltpu
from jax.sharding import PartitionSpec as P

MESH = pl.DeviceIdType.MESH
NY, NX, NZ = 8, 4, 3
NZL = 4
LEV, COLS, NCO = 120, 2048, 64
LG = 16
TILE, NNZ = 128, 4
CH = 512
OC = 256
bf16, f32 = jnp.bfloat16, jnp.float32


def nt(a, b):
    return lax.dot_general(a, b, (((1,), (1,)), ((), ())), preferred_element_type=f32)


def halves(a, b):
    lo = jnp.concatenate([a[:, :NCO], b[:, :NCO]], axis=1)
    hi = jnp.concatenate([a[:, NCO:], b[:, NCO:]], axis=1)
    return lo, hi


def kernel(
    mem_hbm, inc_hbm, vert_ref, tiles_hbm, cols_ref, co_ref, out_ref,
    mem, inc, tl, onehot, s1, r1, s2, r2, blk, s3, r3, pr3, pm, sc, rb,
    in_sem, tl_sem, y_send, y_recv, w_send, w_recv, b_send, b_recv,
    pm_send, pm_recv, p_send, p_recv, c_send, c_recv,
):
    d = lax.axis_index("dom")
    e = lax.axis_index("ens")
    y, x, z = d // (NX * NZ), (d // NZ) % NX, d % NZ
    zl, core = e // 2, e % 2

    def dom(yy, xx, zz):
        return (yy * NX + xx) * NZ + zz

    partner = (d, zl * 2 + 1 - core)
    y_peers = [(y + i) % NY for i in (4, 3, 5, 2, 6, 1, 7)]
    w_peers = [((x + i) % NX, (z + k) % NZ) for i in (2, 1, 3, 0) for k in (1, 2, 0) if i or k]
    b_peers = [((y + i) % NY, (x + k) % NX) for i in (4, 3, 5, 2, 6, 1, 7, 0) for k in (2, 1, 3, 0)]

    steps = COLS // CH
    loads = []
    for i in range(steps):
        at = pl.ds(i * CH, CH)
        a = pltpu.make_async_copy(mem_hbm.at[:, :, at], mem.at[:, :, at], in_sem.at[i, 0])
        b = pltpu.make_async_copy(inc_hbm.at[:, :, at], inc.at[:, :, at], in_sem.at[i, 1])
        a.start()
        b.start()
        loads.append((a, b))

    barrier = pltpu.get_barrier_semaphore()
    greet = [(dom(yy, x, z), e) for yy in y_peers]
    greet += [(dom(y, xx, zz), e) for xx, zz in w_peers]
    greet += [(dom((y + i) % NY, (x + k) % NX, z), e) for i in range(1, NY) for k in range(1, NX)]
    greet += [(d, ((zl + i) % NZL) * 2 + core) for i in range(1, NZL)]
    greet += [partner]
    for peer in greet:
        pl.semaphore_signal(barrier, inc=1, device_id=peer, device_id_type=MESH)

    def tile_load(n):
        dd = dom(n // NX, n % NX, z)
        return pltpu.make_async_copy(
            tiles_hbm.at[dd // 2, :, pl.ds(pl.multiple_of((dd % 2) * NCO, NCO), NCO), :],
            tl.at[n],
            tl_sem,
        )

    def start_tile(n, _):
        tile_load(n).start()
        return 0

    lax.fori_loop(0, NY * NX, start_tile, 0)

    points = lax.broadcasted_iota(jnp.int32, (NCO, COLS), 0)
    onehot[...] = (points == co_ref[...]).astype(f32).astype(bf16)
    sums = [jnp.zeros((LEV, NCO), f32) for _ in range(4)]
    for i in range(steps):
        at = pl.ds(i * CH, CH)
        for a in loads[i]:
            a.wait()
        hot = onehot[:, at]
        for s in range(4):
            w = mem[s, :, at].astype(f32) * inc[s % 2, :, at].astype(f32)
            hi = w.astype(bf16)
            lo = (w - hi.astype(f32)).astype(bf16)
            sums[s] = sums[s] + (nt(hi, hot) + nt(lo, hot))
    summed = jnp.concatenate(sums, axis=1)
    coarse = lax.dot_general(
        vert_ref[...], summed, (((1,), (0,)), ((), ())),
        precision=lax.Precision.HIGHEST, preferred_element_type=f32,
    )
    coarse = jnp.concatenate([coarse, jnp.zeros((NY * LG - LEV, 4 * NCO), f32)], axis=0).astype(bf16)
    for g in range(NY):
        for p in range(2):
            s1[g, p] = coarse[g * LG:(g + 1) * LG, p * 128:(p + 1) * 128]

    pl.semaphore_wait(barrier, len(greet))

    for yy in y_peers:
        pltpu.make_async_remote_copy(
            src_ref=s1.at[yy], dst_ref=r1.at[y], send_sem=y_send, recv_sem=y_recv,
            device_id=(dom(yy, x, z), e), device_id_type=MESH,
        ).start()
    r1[y] = s1[y]
    for q in range(NZL):
        pltpu.make_async_remote_copy(
            src_ref=mem.at[:, :, pl.ds(pl.multiple_of((q * 2 + 1 - core) * OC, OC), OC)],
            dst_ref=pm.at[q], send_sem=pm_send.at[q], recv_sem=pm_recv.at[q],
            device_id=partner, device_id_type=MESH,
        ).start()
    s3[...] = jnp.zeros_like(s3)
    arrived = r1.at[pl.ds(0, NY - 1)]
    pltpu.make_async_copy(arrived, arrived, y_recv).wait()

    for p in range(2):
        for j in range(NY // 2):
            lo, hi = halves(r1[2 * j, p], r1[2 * j + 1, p])
            s2[2 * p, j] = lo
            s2[2 * p + 1, j] = hi
    own = x * NZ + z
    for xx, zz in w_peers:
        pltpu.make_async_remote_copy(
            src_ref=s2.at[xx], dst_ref=r2.at[own], send_sem=w_send, recv_sem=w_recv,
            device_id=(dom(y, xx, zz), e), device_id_type=MESH,
        ).start()
    r2[own] = s2[x]
    arrived = r2.at[pl.ds(0, NX * NZ - 1)]
    pltpu.make_async_copy(arrived, arrived, w_recv).wait()

    for j in range(NY // 2):
        for v in range(NX * NZ // 2):
            lo, hi = halves(r2[2 * v, j], r2[2 * v + 1, j])
            blk[2 * j * (NX * NZ // 2) + v] = lo
            blk[(2 * j + 1) * (NX * NZ // 2) + v] = hi
    pltpu.make_async_copy(tl, tl, tl_sem).wait()
    slot = x * NY + y
    for yy, xx in b_peers:
        n = yy * NX + xx
        b = dom(yy, xx, z) // 2
        picked = jnp.concatenate([blk[cols_ref[b, t]] for t in range(NNZ)], axis=1)
        matrix = jnp.concatenate([tl[n, t] for t in range(NNZ)], axis=1)
        s3[n, :, :NCO] = nt(picked, matrix).astype(bf16)
        if (yy, xx) is not b_peers[-1]:
            pass
    for yy, xx in b_peers[:-1]:
        pltpu.make_async_remote_copy(
            src_ref=s3.at[yy * NX + xx], dst_ref=r3.at[slot], send_sem=b_send, recv_sem=b_recv,
            device_id=(dom(yy, xx, z), e), device_id_type=MESH,
        ).start()
    r3[slot] = s3[y * NX + x]
    arrived = r3.at[pl.ds(0, NY * NX - 1)]
    pltpu.make_async_copy(arrived, arrived, b_recv).wait()

    swap = pltpu.make_async_remote_copy(
        src_ref=r3, dst_ref=pr3, send_sem=p_send, recv_sem=p_recv,
        device_id=partner, device_id_type=MESH,
    )
    swap.start()

    def term(s, fields, local, hot):
        lhs = local[s * NY:(s + 1) * NY].reshape(NY * LG, 128)[:, :NCO]
        back = jnp.dot(lhs, hot, preferred_element_type=f32)
        return fields.astype(f32) * back[:LEV]

    far = zl // 2
    targets = [3 * (1 - far), 2 - far, zl + 1 - 2 * (zl % 2), zl]
    kept = None
    for i, q in enumerate(targets):
        at = pl.ds(pl.multiple_of((q * 2 + core) * OC, OC), OC)
        hot = onehot[:, at]
        parts = [sum(term(k * 2 + c, mem[k * 2 + c, :, at], r3, hot) for k in range(2)) for c in range(2)]
        if i == 0:
            swap.wait_recv()
            for j in range(NZL):
                pltpu.make_async_copy(pm.at[j], pm.at[j], pm_recv.at[j]).wait()
        for c in range(2):
            parts[c] = parts[c] + sum(term(k * 2 + c, pm[q, k * 2 + c], pr3, hot) for k in range(2))
        both = jnp.concatenate(parts, axis=0)
        if i < NZL - 1:
            sc[i] = both.astype(bf16)
            pltpu.make_async_remote_copy(
                src_ref=sc.at[i], dst_ref=rb.at[zl], send_sem=c_send.at[i], recv_sem=c_recv.at[zl],
                device_id=(d, q * 2 + core), device_id_type=MESH,
            ).start()
        else:
            kept = both
    for i in (1, 3, 2):
        j = (zl + i) % NZL
        pltpu.make_async_copy(rb.at[j], rb.at[j], c_recv.at[j]).wait()
        kept = kept + rb[j].astype(f32)
    kept = (kept / 15.0).astype(bf16)
    out_ref[0] = kept[:LEV]
    out_ref[1] = kept[LEV:]

    for ref, count, sem in ((r1, NY - 1, y_send), (r2, NX * NZ - 1, w_send), (r3, NY * NX - 1, b_send)):
        sent = ref.at[pl.ds(0, count)]
        pltpu.make_async_copy(sent, sent, sem).wait()
    for q in range(NZL):
        pltpu.make_async_copy(pm.at[q], pm.at[q], pm_send.at[q]).wait()
    swap.wait_send()
    for i in range(NZL - 1):
        pltpu.make_async_copy(sc.at[i], sc.at[i], c_send.at[i]).wait()


def shards(members, increment, vert_loc, tiles, tile_cols, coarse_of):
    dma = pltpu.SemaphoreType.DMA
    vmem = pl.BlockSpec(memory_space=pltpu.VMEM)
    hbm = pl.BlockSpec(memory_space=pl.ANY)
    return pl.pallas_call(
        kernel,
        name="covary",
        out_shape=jax.ShapeDtypeStruct((2, LEV, OC), bf16),
        in_specs=[hbm, hbm, vmem, hbm, pl.BlockSpec(memory_space=pltpu.SMEM), vmem],
        out_specs=vmem,
        scratch_shapes=[
            pltpu.VMEM((4, LEV, COLS), bf16),
            pltpu.VMEM((2, LEV, COLS), bf16),
            pltpu.VMEM((NY * NX, NNZ, NCO, TILE), bf16),
            pltpu.VMEM((NCO, COLS), bf16),
            pltpu.VMEM((NY, 2, LG, 128), bf16),
            pltpu.VMEM((NY, 2, LG, 128), bf16),
            pltpu.VMEM((NX, NY // 2, LG, 128), bf16),
            pltpu.VMEM((NX * NZ, NY // 2, LG, 128), bf16),
            pltpu.VMEM((NY * NX * NZ // 2, LG, 128), bf16),
            pltpu.VMEM((NY * NX, LG, 128), bf16),
            pltpu.VMEM((NY * NX, LG, 128), bf16),
            pltpu.VMEM((NY * NX, LG, 128), bf16),
            pltpu.VMEM((NZL, 4, LEV, OC), bf16),
            pltpu.VMEM((NZL - 1, 2 * LEV, OC), bf16),
            pltpu.VMEM((NZL, 2 * LEV, OC), bf16),
            dma((COLS // CH, 2)), dma,
            dma, dma, dma, dma, dma, dma,
            dma((NZL,)), dma((NZL,)), dma, dma, dma((NZL - 1,)), dma((NZL,)),
        ],
        compiler_params=pltpu.CompilerParams(
            collective_id=0, has_side_effects=True, vmem_limit_bytes=40 * 2**20
        ),
    )(
        members.reshape(4, LEV, COLS), increment, vert_loc, tiles, tile_cols,
        coarse_of.reshape(1, COLS),
    )


def solution(mesh):
    return jax.shard_map(
        shards,
        mesh=mesh,
        in_specs=(P("ens", None, None, "dom"), P(None, None, "dom"), P(), P(), P(), P("dom")),
        out_specs=P(None, None, ("dom", "ens")),
        check_vma=False,
    )
```

time: 135 us -> 62.3 us (0.46); the launches traced: 133 us -> 61.9 us
  Pallas kernels: 0 us -> 53.4 us
  waiting for transfers between devices: 52.3 us -> 0 us
  starting transfers between devices: 23.8 us -> 0 us
  blocking collectives: 20.1 us -> 0 us
  matrix products: 15.2 us -> 0 us
  between operations: 13.6 us -> 0.01 us
  local copies, waits for them, and re-layouts: 3.71 us -> 8.47 us
  other arithmetic: 4.18 us -> 0 us
    pallas_call x0 -> x1, Pallas kernels: none -> 53.4 us  [shards(): pl.pallas_call(kernel, name='covary', out_shape=jax.ShapeDtypeStruct((2,...]
    reduce_scatter x1 -> x0, waiting for transfers between devices: 39.1 us -> none  [shards(): total = lax.psum_scatter(terms, 'ens', scatter_dimension=2, tiled=True)]
    all_to_all x1 -> x0, starting transfers between devices: 23.8 us -> none  [shards(): lax.all_to_all(coarse, 'dom', split_axis=0, concat_axis=1, tiled=True)]
    all_to_all x1 -> x0, blocking collectives: 20.1 us -> none  [shards(): lax.all_to_all(smoothed, 'dom', split_axis=1, concat_axis=0, tiled=True)]
    dot_general x4 -> x0, matrix products: 15.2 us -> none  [the longest x1 5.26 us: shards(): jnp.einsum('lm,kcmn->kcln', vert_loc, weighted, precision=highest)]
    all_to_all x1 -> x0, waiting for transfers between devices: 13.2 us -> none  [shards(): lax.all_to_all(coarse, 'dom', split_axis=0, concat_axis=1, tiled=True)]
    unnamed x12, local copies, waits for them, and re-layouts: 1.56 us -> 8.47 us
    convert_element_type x2 -> x0, other arithmetic: 3.17 us -> none  [the longest x1 1.61 us: shards(): return (total / (total_mem - 1)).astype(jnp.bfloat16)]
  transfers between devices with their start and end apart: 2 -> 0, of which waited for: 2 -> 0; matrix products, arithmetic and copies ran while one was open for 0% -> 0% of each run, Pallas kernels for 0% -> 0%
where the time goes in v1:
time: 62.3 us; the launch traced here: 61.9 us
  Pallas kernels  53.4 us (86%)
  local copies, waits for them, and re-layouts  8.47 us (14%)
    pallas_call x1, Pallas kernels, shards(): pl.pallas_call(kernel, name='covary', out_shape=jax.ShapeDtypeStruct((2,...  53.4 us
    unnamed x12, local copies, waits for them, and re-layouts  8.47 us

profile of v1, /device:TPU:1, one launch (start us, length us, event | category | flops | bytes accessed | tf_op | source)
XLA Modules:
  0.0 61.9 jit_solution(15276811585515824283)
XLA Ops:
  0.0 0.8 %copy.7.cols_ref = s32[48,4]{1,0:T(8,128)S(1)} copy(s32[48,4]{0,1:T(4,128)} %param.10) | data formatting | bytes 1536 | tf_op args[4]
  0.8 0.0 copy-start
  0.8 2.8 %copy-done = bf16[48,4,128,128]{3,2,1,0:T(8,128)(2,1)S(1)} copy-done((bf16[48,4,128,128]{3,2,1,0:T(8,128)(2,1)S(1)}, bf16[48,4,128,128]{3,2,1,0:T(8,128)(2,1)}, u32[]{:S(2)}) %copy-start) | copy-done | bytes 6291480
  3.6 0.0 copy-start.1
  3.6 1.5 %copy-done.1 = bf16[2,2,120,2048]{3,2,1,0:T(8,128)(2,1)S(1)} copy-done((bf16[2,2,120,2048]{3,2,1,0:T(8,128)(2,1)S(1)}, bf16[2,2,120,2048]{3,2,1,0:T(8,128)(2,1)}, u32[]{:S(2)}) %copy-start.1) | copy-done | bytes 1966104
  5.1 0.0 copy-start.2
  5.1 1.2 %copy-done.2 = bf16[2,120,2048]{2,1,0:T(8,128)(2,1)S(1)} copy-done((bf16[2,120,2048]{2,1,0:T(8,128)(2,1)S(1)}, bf16[2,120,2048]{2,1,0:T(8,128)(2,1)}, u32[]{:S(2)}) %copy-start.2) | copy-done | bytes 983064
  6.3 0.0 copy-start.3
  6.3 0.8 %copy-done.3 = f32[120,120]{1,0:T(8,128)S(1)} copy-done((f32[120,120]{1,0:T(8,128)S(1)}, f32[120,120]{1,0:T(8,128)}, u32[]{:S(2)}) %copy-start.3) | copy-done | bytes 57624
  7.1 0.0 copy-start.4
  7.1 0.7 %copy-done.4 = s32[2048]{0:T(1024)S(1)} copy-done((s32[2048]{0:T(1024)S(1)}, s32[2048]{0:T(1024)}, u32[]{:S(2)}) %copy-start.4) | copy-done | bytes 8216
  7.8 53.4 %covary.1 = bf16[2,120,256]{2,1,0:T(8,128)(2,1)S(1)} custom-call(bf16[4,120,2048]{2,1,0:T(8,128)(2,1)S(1)} %bitcast.2, bf16[2,120,2048]{2,1,0:T(8,128)(2,1)S(1)} %copy-done.2, f32[120,120]{1,0:T(8,128)S(1)} %copy-done.3, bf16[48,4,128,128]{3,2,1,0:T(8,128)(2,1)S(1)} %copy-done, s32[48,4]{1,0:T(8,128)S(1)} %copy.7.cols_ref, s32[1,2048]{1,0:T(1,128)S(1)} %bitcast.3), custom_call_target="tpu_custom_call" | custom-call | tf_op jit(solution)/shard_map/covary/pallas_call | solution.py:216
  61.3 0.7 %copy.9 = bf16[2,120,256]{2,1,0:T(8,128)(2,1)} copy(bf16[2,120,256]{2,1,0:T(8,128)(2,1)S(1)} %covary.1) | data formatting | bytes 245760
Async XLA Ops:
  0.8 2.8 %copy-start = (bf16[48,4,128,128]{3,2,1,0:T(8,128)(2,1)S(1)}, bf16[48,4,128,128]{3,2,1,0:T(8,128)(2,1)}, u32[]{:S(2)}) copy-start(bf16[48,4,128,128]{3,2,1,0:T(8,128)(2,1)} %tiles_hbm.1) | copy-start | bytes 18874372
  3.6 1.5 %copy-start.1 = (bf16[2,2,120,2048]{3,2,1,0:T(8,128)(2,1)S(1)}, bf16[2,2,120,2048]{3,2,1,0:T(8,128)(2,1)}, u32[]{:S(2)}) copy-start(bf16[2,2,120,2048]{3,2,1,0:T(8,128)(2,1)} %param.6) | copy-start | bytes 5898244
  5.1 1.2 %copy-start.2 = (bf16[2,120,2048]{2,1,0:T(8,128)(2,1)S(1)}, bf16[2,120,2048]{2,1,0:T(8,128)(2,1)}, u32[]{:S(2)}) copy-start(bf16[2,120,2048]{2,1,0:T(8,128)(2,1)} %inc_hbm.1) | copy-start | bytes 2949124
  6.3 0.8 %copy-start.3 = (f32[120,120]{1,0:T(8,128)S(1)}, f32[120,120]{1,0:T(8,128)}, u32[]{:S(2)}) copy-start(f32[120,120]{1,0:T(8,128)} %vert_ref.1) | copy-start | bytes 172804
  7.1 0.7 %copy-start.4 = (s32[2048]{0:T(1024)S(1)}, s32[2048]{0:T(1024)}, u32[]{:S(2)}) copy-start(s32[2048]{0:T(1024)} %param.11) | copy-start | bytes 24580

commit v2 on v1

--- a/solution.py
+++ b/solution.py
@@ -27,9 +27,9 @@
 
 
 def kernel(
-    mem_hbm, inc_hbm, vert_ref, tiles_hbm, cols_ref, co_ref, out_ref,
-    mem, inc, tl, onehot, s1, r1, s2, r2, blk, s3, r3, pr3, pm, sc, rb,
-    in_sem, tl_sem, y_send, y_recv, w_send, w_recv, b_send, b_recv,
+    mem_hbm, inc_hbm, vert_hbm, tiles_hbm, cols_hbm, co_hbm, out_ref,
+    vert_ref, cols_ref, co_ref, mem, inc, tl, onehot, s1, r1, s2, r2, blk, s3, r3, pr3, pm, sc, rb,
+    small_sem, in_sem, tl_sem, y_send, y_recv, w_send, w_recv, b_send, b_recv,
     pm_send, pm_recv, p_send, p_recv, c_send, c_recv,
 ):
     d = lax.axis_index("dom")
@@ -45,6 +45,12 @@
     w_peers = [((x + i) % NX, (z + k) % NZ) for i in (2, 1, 3, 0) for k in (1, 2, 0) if i or k]
     b_peers = [((y + i) % NY, (x + k) % NX) for i in (4, 3, 5, 2, 6, 1, 7, 0) for k in (2, 1, 3, 0)]
 
+    small = [
+        pltpu.make_async_copy(src, dst, small_sem.at[i])
+        for i, (src, dst) in enumerate(((co_hbm, co_ref), (vert_hbm, vert_ref), (cols_hbm, cols_ref)))
+    ]
+    for copy in small:
+        copy.start()
     steps = COLS // CH
     loads = []
     for i in range(steps):
@@ -78,6 +84,7 @@
 
     lax.fori_loop(0, NY * NX, start_tile, 0)
 
+    small[0].wait()
     points = lax.broadcasted_iota(jnp.int32, (NCO, COLS), 0)
     onehot[...] = (points == co_ref[...]).astype(f32).astype(bf16)
     sums = [jnp.zeros((LEV, NCO), f32) for _ in range(4)]
@@ -91,6 +98,7 @@
             hi = w.astype(bf16)
             lo = (w - hi.astype(f32)).astype(bf16)
             sums[s] = sums[s] + (nt(hi, hot) + nt(lo, hot))
+    small[1].wait()
     summed = jnp.concatenate(sums, axis=1)
     coarse = lax.dot_general(
         vert_ref[...], summed, (((1,), (0,)), ((), ())),
@@ -109,12 +117,6 @@
             device_id=(dom(yy, x, z), e), device_id_type=MESH,
         ).start()
     r1[y] = s1[y]
-    for q in range(NZL):
-        pltpu.make_async_remote_copy(
-            src_ref=mem.at[:, :, pl.ds(pl.multiple_of((q * 2 + 1 - core) * OC, OC), OC)],
-            dst_ref=pm.at[q], send_sem=pm_send.at[q], recv_sem=pm_recv.at[q],
-            device_id=partner, device_id_type=MESH,
-        ).start()
     s3[...] = jnp.zeros_like(s3)
     arrived = r1.at[pl.ds(0, NY - 1)]
     pltpu.make_async_copy(arrived, arrived, y_recv).wait()
@@ -131,6 +133,12 @@
             device_id=(dom(y, xx, zz), e), device_id_type=MESH,
         ).start()
     r2[own] = s2[x]
+    for q in range(NZL):
+        pltpu.make_async_remote_copy(
+            src_ref=mem.at[:, :, pl.ds(pl.multiple_of((q * 2 + 1 - core) * OC, OC), OC)],
+            dst_ref=pm.at[q], send_sem=pm_send.at[q], recv_sem=pm_recv.at[q],
+            device_id=partner, device_id_type=MESH,
+        ).start()
     arrived = r2.at[pl.ds(0, NX * NZ - 1)]
     pltpu.make_async_copy(arrived, arrived, w_recv).wait()
 
@@ -140,15 +148,14 @@
             blk[2 * j * (NX * NZ // 2) + v] = lo
             blk[(2 * j + 1) * (NX * NZ // 2) + v] = hi
     pltpu.make_async_copy(tl, tl, tl_sem).wait()
+    small[2].wait()
     slot = x * NY + y
     for yy, xx in b_peers:
         n = yy * NX + xx
         b = dom(yy, xx, z) // 2
-        picked = jnp.concatenate([blk[cols_ref[b, t]] for t in range(NNZ)], axis=1)
+        picked = jnp.concatenate([blk[cols_ref[t, b]] for t in range(NNZ)], axis=1)
         matrix = jnp.concatenate([tl[n, t] for t in range(NNZ)], axis=1)
         s3[n, :, :NCO] = nt(picked, matrix).astype(bf16)
-        if (yy, xx) is not b_peers[-1]:
-            pass
     for yy, xx in b_peers[:-1]:
         pltpu.make_async_remote_copy(
             src_ref=s3.at[yy * NX + xx], dst_ref=r3.at[slot], send_sem=b_send, recv_sem=b_recv,
@@ -217,9 +224,12 @@
         kernel,
         name="covary",
         out_shape=jax.ShapeDtypeStruct((2, LEV, OC), bf16),
-        in_specs=[hbm, hbm, vmem, hbm, pl.BlockSpec(memory_space=pltpu.SMEM), vmem],
+        in_specs=[hbm] * 6,
         out_specs=vmem,
         scratch_shapes=[
+            pltpu.VMEM((LEV, LEV), f32),
+            pltpu.SMEM((NNZ, NY * NX * NZ // 2), jnp.int32),
+            pltpu.VMEM((1, COLS), jnp.int32),
             pltpu.VMEM((4, LEV, COLS), bf16),
             pltpu.VMEM((2, LEV, COLS), bf16),
             pltpu.VMEM((NY * NX, NNZ, NCO, TILE), bf16),
@@ -235,15 +245,15 @@
             pltpu.VMEM((NZL, 4, LEV, OC), bf16),
             pltpu.VMEM((NZL - 1, 2 * LEV, OC), bf16),
             pltpu.VMEM((NZL, 2 * LEV, OC), bf16),
-            dma((COLS // CH, 2)), dma,
+            dma((3,)), dma((COLS // CH, 2)), dma,
             dma, dma, dma, dma, dma, dma,
             dma((NZL,)), dma((NZL,)), dma, dma, dma((NZL - 1,)), dma((NZL,)),
         ],
         compiler_params=pltpu.CompilerParams(
-            collective_id=0, has_side_effects=True, vmem_limit_bytes=40 * 2**20
+            collective_id=0, has_side_effects=True, vmem_limit_bytes=63 * 2**20
         ),
     )(
-        members.reshape(4, LEV, COLS), increment, vert_loc, tiles, tile_cols,
+        members.reshape(4, LEV, COLS), increment, vert_loc, tiles, tile_cols.T,
         coarse_of.reshape(1, COLS),
     )
 

time: 62.3 us -> 54.5 us (0.87)
  local copies, waits for them, and re-layouts: 8.47 us -> 1.56 us
    unnamed x12 -> x1, local copies, waits for them, and re-layouts: 8.47 us -> 1.56 us
    pallas_call x1, Pallas kernels: 53.4 us -> 52.8 us  [shards(): pl.pallas_call(kernel, name='covary', out_shape=jax.ShapeDtypeStruct((2,...]
where the time goes in v2:
time: 54.5 us; the launch traced here: 54.3 us
  Pallas kernels  52.8 us (97%)
  local copies, waits for them, and re-layouts  1.56 us (3%)
    pallas_call x1, Pallas kernels, shards(): pl.pallas_call(kernel, name='covary', out_shape=jax.ShapeDtypeStruct((2,...  52.8 us
    unnamed x1, local copies, waits for them, and re-layouts  1.56 us

profile of v2, /device:TPU:1, one launch (start us, length us, event | category | flops | bytes accessed | tf_op | source)
XLA Modules:
  0.0 54.3 jit_solution(16623748241268379151)
XLA Ops:
  0.0 52.8 %covary.1 = bf16[2,120,256]{2,1,0:T(8,128)(2,1)} custom-call(bf16[4,120,2048]{2,1,0:T(8,128)(2,1)} %bitcast.3, bf16[2,120,2048]{2,1,0:T(8,128)(2,1)} %inc_hbm.1, f32[120,120]{1,0:T(8,128)} %vert_hbm.1, bf16[48,4,128,128]{3,2,1,0:T(8,128)(2,1)} %tiles_hbm.1, s32[4,48]{1,0:T(4,128)} %bitcast.5, s32[1,2048]{1,0:T(1,128)} %bitcast.4), custom_call_target="tpu_custom_call" | custom-call | tf_op jit(solution)/shard_map/covary/pallas_call | solution.py:223
  52.8 1.6 %copy.8 = bf16[2,120,256]{2,1,0:T(8,128)(2,1)} copy(bf16[2,120,256]{2,1,0:T(8,128)(2,1)} %covary.1) | data formatting | bytes 245760

commit v3 on v2

--- a/solution.py
+++ b/solution.py
@@ -30,7 +30,7 @@
     mem_hbm, inc_hbm, vert_hbm, tiles_hbm, cols_hbm, co_hbm, out_ref,
     vert_ref, cols_ref, co_ref, mem, inc, tl, onehot, s1, r1, s2, r2, blk, s3, r3, pr3, pm, sc, rb,
     small_sem, in_sem, tl_sem, y_send, y_recv, w_send, w_recv, b_send, b_recv,
-    pm_send, pm_recv, p_send, p_recv, c_send, c_recv,
+    pm_send, pm_recv, p_send, p_recv, c_send, c_recv, ready,
 ):
     d = lax.axis_index("dom")
     e = lax.axis_index("ens")
@@ -63,8 +63,8 @@
 
     barrier = pltpu.get_barrier_semaphore()
     greet = [(dom(yy, x, z), e) for yy in y_peers]
-    greet += [(dom(y, xx, zz), e) for xx, zz in w_peers]
-    greet += [(dom((y + i) % NY, (x + k) % NX, z), e) for i in range(1, NY) for k in range(1, NX)]
+    greet += [(dom(y, (x + i) % NX, z), e) for i in range(1, NX)]
+    greet += [(dom(y, x, (z + i) % NZ), e) for i in range(1, NZ)]
     greet += [(d, ((zl + i) % NZL) * 2 + core) for i in range(1, NZL)]
     greet += [partner]
     for peer in greet:
@@ -117,6 +117,8 @@
             device_id=(dom(yy, x, z), e), device_id_type=MESH,
         ).start()
     r1[y] = s1[y]
+    for i in range(1, NX):
+        pl.semaphore_signal(ready, inc=1, device_id=(dom(y, (x + i) % NX, z), e), device_id_type=MESH)
     s3[...] = jnp.zeros_like(s3)
     arrived = r1.at[pl.ds(0, NY - 1)]
     pltpu.make_async_copy(arrived, arrived, y_recv).wait()
@@ -127,6 +129,7 @@
             s2[2 * p, j] = lo
             s2[2 * p + 1, j] = hi
     own = x * NZ + z
+    pl.semaphore_wait(ready, NX - 1)
     for xx, zz in w_peers:
         pltpu.make_async_remote_copy(
             src_ref=s2.at[xx], dst_ref=r2.at[own], send_sem=w_send, recv_sem=w_recv,
@@ -150,17 +153,19 @@
     pltpu.make_async_copy(tl, tl, tl_sem).wait()
     small[2].wait()
     slot = x * NY + y
-    for yy, xx in b_peers:
-        n = yy * NX + xx
-        b = dom(yy, xx, z) // 2
-        picked = jnp.concatenate([blk[cols_ref[t, b]] for t in range(NNZ)], axis=1)
-        matrix = jnp.concatenate([tl[n, t] for t in range(NNZ)], axis=1)
-        s3[n, :, :NCO] = nt(picked, matrix).astype(bf16)
-    for yy, xx in b_peers[:-1]:
-        pltpu.make_async_remote_copy(
-            src_ref=s3.at[yy * NX + xx], dst_ref=r3.at[slot], send_sem=b_send, recv_sem=b_recv,
-            device_id=(dom(yy, xx, z), e), device_id_type=MESH,
-        ).start()
+    for g in range(0, NY * NX, 8):
+        group = b_peers[g:g + 8]
+        for yy, xx in group:
+            n = yy * NX + xx
+            b = dom(yy, xx, z) // 2
+            picked = jnp.concatenate([blk[cols_ref[t, b]] for t in range(NNZ)], axis=1)
+            matrix = jnp.concatenate([tl[n, t] for t in range(NNZ)], axis=1)
+            s3[n, :, :NCO] = nt(picked, matrix).astype(bf16)
+        for yy, xx in group[:NY * NX - 1 - g]:
+            pltpu.make_async_remote_copy(
+                src_ref=s3.at[yy * NX + xx], dst_ref=r3.at[slot], send_sem=b_send, recv_sem=b_recv,
+                device_id=(dom(yy, xx, z), e), device_id_type=MESH,
+            ).start()
     r3[slot] = s3[y * NX + x]
     arrived = r3.at[pl.ds(0, NY * NX - 1)]
     pltpu.make_async_copy(arrived, arrived, b_recv).wait()
@@ -248,6 +253,7 @@
             dma((3,)), dma((COLS // CH, 2)), dma,
             dma, dma, dma, dma, dma, dma,
             dma((NZL,)), dma((NZL,)), dma, dma, dma((NZL - 1,)), dma((NZL,)),
+            pltpu.SemaphoreType.REGULAR,
         ],
         compiler_params=pltpu.CompilerParams(
             collective_id=0, has_side_effects=True, vmem_limit_bytes=63 * 2**20

time: 54.5 us -> 52.2 us (0.958)
  Pallas kernels: 52.8 us -> 50.5 us
    pallas_call x1, Pallas kernels: 52.8 us -> 50.5 us  [shards(): pl.pallas_call(kernel, name='covary', out_shape=jax.ShapeDtypeStruct((2,...]
where the time goes in v3:
time: 52.2 us; the launch traced here: 52.1 us
  Pallas kernels  50.5 us (97%)
  local copies, waits for them, and re-layouts  1.56 us (3%)
    pallas_call x1, Pallas kernels, shards(): pl.pallas_call(kernel, name='covary', out_shape=jax.ShapeDtypeStruct((2,...  50.5 us
    unnamed x1, local copies, waits for them, and re-layouts  1.56 us

profile of v3, /device:TPU:1, one launch (start us, length us, event | category | flops | bytes accessed | tf_op | source)
XLA Modules:
  0.0 52.1 jit_solution(7620590162743305252)
XLA Ops:
  0.0 50.5 %covary.1 = bf16[2,120,256]{2,1,0:T(8,128)(2,1)} custom-call(bf16[4,120,2048]{2,1,0:T(8,128)(2,1)} %bitcast.3, bf16[2,120,2048]{2,1,0:T(8,128)(2,1)} %inc_hbm.1, f32[120,120]{1,0:T(8,128)} %vert_hbm.1, bf16[48,4,128,128]{3,2,1,0:T(8,128)(2,1)} %tiles_hbm.1, s32[4,48]{1,0:T(4,128)} %bitcast.5, s32[1,2048]{1,0:T(1,128)} %bitcast.4), custom_call_target="tpu_custom_call" | custom-call | tf_op jit(solution)/shard_map/covary/pallas_call | solution.py:228
  50.5 1.6 %copy.8 = bf16[2,120,256]{2,1,0:T(8,128)(2,1)} copy(bf16[2,120,256]{2,1,0:T(8,128)(2,1)} %covary.1) | data formatting | bytes 245760

commit v4 on v3

--- a/solution.py
+++ b/solution.py
@@ -119,9 +119,19 @@
     r1[y] = s1[y]
     for i in range(1, NX):
         pl.semaphore_signal(ready, inc=1, device_id=(dom(y, (x + i) % NX, z), e), device_id_type=MESH)
-    s3[...] = jnp.zeros_like(s3)
     arrived = r1.at[pl.ds(0, NY - 1)]
     pltpu.make_async_copy(arrived, arrived, y_recv).wait()
+
+    def sent_to(zz):
+        @pl.when(z != zz)
+        def _():
+            sent = r2.at[pl.ds(0, NX)]
+            pltpu.make_async_copy(sent, sent, w_send.at[zz]).wait()
+
+        @pl.when(z == zz)
+        def _():
+            sent = r2.at[pl.ds(0, NX - 1)]
+            pltpu.make_async_copy(sent, sent, w_send.at[zz]).wait()
 
     for p in range(2):
         for j in range(NY // 2):
@@ -130,11 +140,19 @@
             s2[2 * p + 1, j] = hi
     own = x * NZ + z
     pl.semaphore_wait(ready, NX - 1)
-    for xx, zz in w_peers:
-        pltpu.make_async_remote_copy(
-            src_ref=s2.at[xx], dst_ref=r2.at[own], send_sem=w_send, recv_sem=w_recv,
-            device_id=(dom(y, xx, zz), e), device_id_type=MESH,
-        ).start()
+    for zz in range(NZ):
+        for i in (2, 1, 3, 0):
+            xx = (x + i) % NX
+            copy = pltpu.make_async_remote_copy(
+                src_ref=s2.at[xx], dst_ref=r2.at[own], send_sem=w_send.at[zz], recv_sem=w_recv,
+                device_id=(dom(y, xx, zz), e), device_id_type=MESH,
+            )
+            if i:
+                copy.start()
+            else:
+                pl.when(z != zz)(copy.start)
+        if zz == 0:
+            sent_to(zz)
     r2[own] = s2[x]
     for q in range(NZL):
         pltpu.make_async_remote_copy(
@@ -160,26 +178,39 @@
             b = dom(yy, xx, z) // 2
             picked = jnp.concatenate([blk[cols_ref[t, b]] for t in range(NNZ)], axis=1)
             matrix = jnp.concatenate([tl[n, t] for t in range(NNZ)], axis=1)
-            s3[n, :, :NCO] = nt(picked, matrix).astype(bf16)
-        for yy, xx in group[:NY * NX - 1 - g]:
+            smooth = nt(picked, matrix)
+            s3[n] = jnp.concatenate([smooth[:LG // 2], smooth[LG // 2:]], axis=1).astype(bf16)
+        for peer in group:
+            yy, xx = peer
+            if peer is not b_peers[-1]:
+                pltpu.make_async_remote_copy(
+                    src_ref=s3.at[yy * NX + xx], dst_ref=r3.at[slot], send_sem=b_send, recv_sem=b_recv,
+                    device_id=(dom(yy, xx, z), e), device_id_type=MESH,
+                ).start()
             pltpu.make_async_remote_copy(
-                src_ref=s3.at[yy * NX + xx], dst_ref=r3.at[slot], send_sem=b_send, recv_sem=b_recv,
-                device_id=(dom(yy, xx, z), e), device_id_type=MESH,
+                src_ref=s3.at[yy * NX + xx], dst_ref=pr3.at[slot], send_sem=p_send, recv_sem=p_recv,
+                device_id=(dom(yy, xx, z), zl * 2 + 1 - core), device_id_type=MESH,
             ).start()
     r3[slot] = s3[y * NX + x]
     arrived = r3.at[pl.ds(0, NY * NX - 1)]
     pltpu.make_async_copy(arrived, arrived, b_recv).wait()
-
-    swap = pltpu.make_async_remote_copy(
-        src_ref=r3, dst_ref=pr3, send_sem=p_send, recv_sem=p_recv,
-        device_id=partner, device_id_type=MESH,
-    )
-    swap.start()
-
-    def term(s, fields, local, hot):
-        lhs = local[s * NY:(s + 1) * NY].reshape(NY * LG, 128)[:, :NCO]
-        back = jnp.dot(lhs, hot, preferred_element_type=f32)
-        return fields.astype(f32) * back[:LEV]
+    pltpu.make_async_copy(pr3, pr3, p_recv).wait()
+    for j in range(NZL):
+        pltpu.make_async_copy(pm.at[j], pm.at[j], pm_recv.at[j]).wait()
+
+    def rows(field):
+        tiles = [field[g * 8:(g + 1) * 8] for g in range(LEV // 8)]
+        return jnp.concatenate(tiles[0::2] + tiles[1::2], axis=0)
+
+    def packed(ref, s):
+        return ref[s * NY:(s + 1) * NY].astype(f32).reshape(NY * LG // 2, 128).astype(bf16)
+
+    local = [packed(r3, s) for s in range(4)] + [packed(pr3, s) for s in range(4)]
+    none = jnp.zeros((NCO, OC), bf16)
+
+    def term(s, field, hot):
+        back = [jnp.dot(local[s], h, preferred_element_type=f32) for h in hot]
+        return rows(field.astype(f32)) * jnp.concatenate(back, axis=0)[:LEV]
 
     far = zl // 2
     targets = [3 * (1 - far), 2 - far, zl + 1 - 2 * (zl % 2), zl]
@@ -187,13 +218,12 @@
     for i, q in enumerate(targets):
         at = pl.ds(pl.multiple_of((q * 2 + core) * OC, OC), OC)
         hot = onehot[:, at]
-        parts = [sum(term(k * 2 + c, mem[k * 2 + c, :, at], r3, hot) for k in range(2)) for c in range(2)]
-        if i == 0:
-            swap.wait_recv()
-            for j in range(NZL):
-                pltpu.make_async_copy(pm.at[j], pm.at[j], pm_recv.at[j]).wait()
-        for c in range(2):
-            parts[c] = parts[c] + sum(term(k * 2 + c, pm[q, k * 2 + c], pr3, hot) for k in range(2))
+        hot = jnp.concatenate([hot, none], axis=0), jnp.concatenate([none, hot], axis=0)
+        parts = [
+            sum(term(k * 2 + c, mem[k * 2 + c, :, at], hot) for k in range(2))
+            + sum(term(4 + k * 2 + c, pm[q, k * 2 + c], hot) for k in range(2))
+            for c in range(2)
+        ]
         both = jnp.concatenate(parts, axis=0)
         if i < NZL - 1:
             sc[i] = both.astype(bf16)
@@ -207,16 +237,21 @@
         j = (zl + i) % NZL
         pltpu.make_async_copy(rb.at[j], rb.at[j], c_recv.at[j]).wait()
         kept = kept + rb[j].astype(f32)
-    kept = (kept / 15.0).astype(bf16)
-    out_ref[0] = kept[:LEV]
-    out_ref[1] = kept[LEV:]
-
-    for ref, count, sem in ((r1, NY - 1, y_send), (r2, NX * NZ - 1, w_send), (r3, NY * NX - 1, b_send)):
+    kept = kept / 15.0
+    for c in range(2):
+        tiles = [kept[c * LEV + g * 8:c * LEV + (g + 1) * 8] for g in range(LEV // 8)]
+        first = (LEV // 8 + 1) // 2
+        order = [tiles[g // 2 + first * (g % 2)] for g in range(LEV // 8)]
+        out_ref[c] = jnp.concatenate(order, axis=0).astype(bf16)
+
+    for ref, count, sem in ((r1, NY - 1, y_send), (r3, NY * NX - 1, b_send)):
         sent = ref.at[pl.ds(0, count)]
         pltpu.make_async_copy(sent, sent, sem).wait()
+    for zz in range(1, NZ):
+        sent_to(zz)
     for q in range(NZL):
         pltpu.make_async_copy(pm.at[q], pm.at[q], pm_send.at[q]).wait()
-    swap.wait_send()
+    pltpu.make_async_copy(pr3, pr3, p_send).wait()
     for i in range(NZL - 1):
         pltpu.make_async_copy(sc.at[i], sc.at[i], c_send.at[i]).wait()
 
@@ -244,14 +279,14 @@
             pltpu.VMEM((NX, NY // 2, LG, 128), bf16),
             pltpu.VMEM((NX * NZ, NY // 2, LG, 128), bf16),
             pltpu.VMEM((NY * NX * NZ // 2, LG, 128), bf16),
-            pltpu.VMEM((NY * NX, LG, 128), bf16),
-            pltpu.VMEM((NY * NX, LG, 128), bf16),
-            pltpu.VMEM((NY * NX, LG, 128), bf16),
+            pltpu.VMEM((NY * NX, LG // 2, 128), bf16),
+            pltpu.VMEM((NY * NX, LG // 2, 128), bf16),
+            pltpu.VMEM((NY * NX, LG // 2, 128), bf16),
             pltpu.VMEM((NZL, 4, LEV, OC), bf16),
             pltpu.VMEM((NZL - 1, 2 * LEV, OC), bf16),
             pltpu.VMEM((NZL, 2 * LEV, OC), bf16),
             dma((3,)), dma((COLS // CH, 2)), dma,
-            dma, dma, dma, dma, dma, dma,
+            dma, dma, dma((NZ,)), dma, dma, dma,
             dma((NZL,)), dma((NZL,)), dma, dma, dma((NZL - 1,)), dma((NZL,)),
             pltpu.SemaphoreType.REGULAR,
         ],

time: 52.2 us -> 51.1 us (0.979); the launches traced: 52.1 us -> 50.3 us
  Pallas kernels: 50.5 us -> 48.7 us
    pallas_call x1, Pallas kernels: 50.5 us -> 48.7 us  [shards(): pl.pallas_call(kernel, name='covary', out_shape=jax.ShapeDtypeStruct((2,...]
where the time goes in v4:
time: 51.1 us; the launch traced here: 50.3 us
  Pallas kernels  48.7 us (95%)
  local copies, waits for them, and re-layouts  1.56 us (3%)
    pallas_call x1, Pallas kernels, shards(): pl.pallas_call(kernel, name='covary', out_shape=jax.ShapeDtypeStruct((2,...  48.7 us
    unnamed x1, local copies, waits for them, and re-layouts  1.56 us

profile of v4, /device:TPU:1, one launch (start us, length us, event | category | flops | bytes accessed | tf_op | source)
XLA Modules:
  0.0 50.3 jit_solution(4778345127986833731)
XLA Ops:
  0.0 48.7 %covary.1 = bf16[2,120,256]{2,1,0:T(8,128)(2,1)} custom-call(bf16[4,120,2048]{2,1,0:T(8,128)(2,1)} %bitcast.3, bf16[2,120,2048]{2,1,0:T(8,128)(2,1)} %inc_hbm.1, f32[120,120]{1,0:T(8,128)} %vert_hbm.1, bf16[48,4,128,128]{3,2,1,0:T(8,128)(2,1)} %tiles_hbm.1, s32[4,48]{1,0:T(4,128)} %bitcast.5, s32[1,2048]{1,0:T(1,128)} %bitcast.4), custom_call_target="tpu_custom_call" | custom-call | tf_op jit(solution)/shard_map/covary/pallas_call | solution.py:263
  48.7 1.6 %copy.8 = bf16[2,120,256]{2,1,0:T(8,128)(2,1)} copy(bf16[2,120,256]{2,1,0:T(8,128)(2,1)} %covary.1) | data formatting | bytes 245760

commit v5 on v4

--- a/solution.py
+++ b/solution.py
@@ -28,8 +28,8 @@
 
 def kernel(
     mem_hbm, inc_hbm, vert_hbm, tiles_hbm, cols_hbm, co_hbm, out_ref,
-    vert_ref, cols_ref, co_ref, mem, inc, tl, onehot, s1, r1, s2, r2, blk, s3, r3, pr3, pm, sc, rb,
-    small_sem, in_sem, tl_sem, y_send, y_recv, w_send, w_recv, b_send, b_recv,
+    vert_ref, cols_ref, co_ref, mem, inc, tl, onehot, s1, ra, blk, s3, r3, pr3, pm, sc, rb,
+    small_sem, in_sem, tl_sem, a_send, d_send, a_recv, z_send, b_send, b_recv,
     pm_send, pm_recv, p_send, p_recv, c_send, c_recv, ready,
 ):
     d = lax.axis_index("dom")
@@ -41,9 +41,10 @@
         return (yy * NX + xx) * NZ + zz
 
     partner = (d, zl * 2 + 1 - core)
-    y_peers = [(y + i) % NY for i in (4, 3, 5, 2, 6, 1, 7)]
-    w_peers = [((x + i) % NX, (z + k) % NZ) for i in (2, 1, 3, 0) for k in (1, 2, 0) if i or k]
-    b_peers = [((y + i) % NY, (x + k) % NX) for i in (4, 3, 5, 2, 6, 1, 7, 0) for k in (2, 1, 3, 0)]
+    peers = [((y + i) % NY, (x + k) % NX) for i in (4, 3, 5, 2, 6, 1, 7, 0) for k in (2, 1, 3, 0)]
+    lines = [((y + i) % NY, x) for i in (4, 3, 5, 2, 6, 1, 7)] + [(y, (x + k) % NX) for k in (2, 1, 3)]
+    rest = [((y + i) % NY, (x + k) % NX) for i in (4, 3, 5, 2, 6, 1, 7) for k in (2, 1, 3)]
+    me = y * NX + x
 
     small = [
         pltpu.make_async_copy(src, dst, small_sem.at[i])
@@ -62,27 +63,26 @@
         loads.append((a, b))
 
     barrier = pltpu.get_barrier_semaphore()
-    greet = [(dom(yy, x, z), e) for yy in y_peers]
-    greet += [(dom(y, (x + i) % NX, z), e) for i in range(1, NX)]
-    greet += [(dom(y, x, (z + i) % NZ), e) for i in range(1, NZ)]
-    greet += [(d, ((zl + i) % NZL) * 2 + core) for i in range(1, NZL)]
-    greet += [partner]
-    for peer in greet:
+
+    def greet(peer):
         pl.semaphore_signal(barrier, inc=1, device_id=peer, device_id_type=MESH)
 
-    def tile_load(n):
-        dd = dom(n // NX, n % NX, z)
-        return pltpu.make_async_copy(
-            tiles_hbm.at[dd // 2, :, pl.ds(pl.multiple_of((dd % 2) * NCO, NCO), NCO), :],
-            tl.at[n],
-            tl_sem,
-        )
-
-    def start_tile(n, _):
-        tile_load(n).start()
-        return 0
-
-    lax.fori_loop(0, NY * NX, start_tile, 0)
+    @pl.when(z == 0)
+    def _():
+        for yy, xx in peers:
+            for zz in range(1, NZ):
+                greet((dom(yy, xx, zz), e))
+
+    for yy, xx in lines:
+        greet((dom(yy, xx, z), e))
+    for i in range(1, NZL):
+        greet((d, ((zl + i) % NZL) * 2 + core))
+    greet(partner)
+
+    @pl.when(z != 0)
+    def _():
+        greet((dom(y, x, 0), e))
+        greet((dom(y, x, NZ - z), e))
 
     small[0].wait()
     points = lax.broadcasted_iota(jnp.int32, (NCO, COLS), 0)
@@ -104,75 +104,81 @@
         vert_ref[...], summed, (((1,), (0,)), ((), ())),
         precision=lax.Precision.HIGHEST, preferred_element_type=f32,
     )
-    coarse = jnp.concatenate([coarse, jnp.zeros((NY * LG - LEV, 4 * NCO), f32)], axis=0).astype(bf16)
+    coarse = jnp.concatenate([coarse, jnp.zeros((NY * LG - LEV, 4 * NCO), f32)], axis=0)
     for g in range(NY):
-        for p in range(2):
-            s1[g, p] = coarse[g * LG:(g + 1) * LG, p * 128:(p + 1) * 128]
-
-    pl.semaphore_wait(barrier, len(greet))
-
-    for yy in y_peers:
+        for s in range(NX):
+            part = coarse[g * LG:(g + 1) * LG, s * NCO:(s + 1) * NCO]
+            s1[g * NX + s] = jnp.concatenate([part[:LG // 2], part[LG // 2:]], axis=1).astype(bf16)
+
+    here = len(lines) + NZL
+
+    @pl.when(z == 0)
+    def _():
+        pl.semaphore_wait(barrier, here + NZ - 1)
+
+    def deal(yy, xx, zz, sem):
         pltpu.make_async_remote_copy(
-            src_ref=s1.at[yy], dst_ref=r1.at[y], send_sem=y_send, recv_sem=y_recv,
-            device_id=(dom(yy, x, z), e), device_id_type=MESH,
+            src_ref=s1.at[yy * NX + xx], dst_ref=ra.at[z, me], send_sem=sem, recv_sem=a_recv.at[z],
+            device_id=(dom(yy, xx, zz), e), device_id_type=MESH,
         ).start()
-    r1[y] = s1[y]
-    for i in range(1, NX):
-        pl.semaphore_signal(ready, inc=1, device_id=(dom(y, (x + i) % NX, z), e), device_id_type=MESH)
-    arrived = r1.at[pl.ds(0, NY - 1)]
-    pltpu.make_async_copy(arrived, arrived, y_recv).wait()
-
-    def sent_to(zz):
-        @pl.when(z != zz)
-        def _():
-            sent = r2.at[pl.ds(0, NX)]
-            pltpu.make_async_copy(sent, sent, w_send.at[zz]).wait()
-
-        @pl.when(z == zz)
-        def _():
-            sent = r2.at[pl.ds(0, NX - 1)]
-            pltpu.make_async_copy(sent, sent, w_send.at[zz]).wait()
-
-    for p in range(2):
-        for j in range(NY // 2):
-            lo, hi = halves(r1[2 * j, p], r1[2 * j + 1, p])
-            s2[2 * p, j] = lo
-            s2[2 * p + 1, j] = hi
-    own = x * NZ + z
+
+    @pl.when(z != 0)
+    def _():
+        pl.semaphore_wait(barrier, here + NY * NX + 1)
+        for yy, xx in peers:
+            deal(yy, xx, 0, d_send)
+
+    for xx in [(x + k) % NX for k in (2, 1, 3)]:
+        pl.semaphore_signal(ready, inc=1, device_id=(dom(y, xx, z), e), device_id_type=MESH)
+    for yy, xx in lines:
+        deal(yy, xx, z, a_send)
+    ra[z, me] = s1[me]
     pl.semaphore_wait(ready, NX - 1)
-    for zz in range(NZ):
-        for i in (2, 1, 3, 0):
-            xx = (x + i) % NX
-            copy = pltpu.make_async_remote_copy(
-                src_ref=s2.at[xx], dst_ref=r2.at[own], send_sem=w_send.at[zz], recv_sem=w_recv,
-                device_id=(dom(y, xx, zz), e), device_id_type=MESH,
-            )
-            if i:
-                copy.start()
-            else:
-                pl.when(z != zz)(copy.start)
-        if zz == 0:
-            sent_to(zz)
-    r2[own] = s2[x]
+    for yy, xx in rest:
+        deal(yy, xx, z, a_send)
     for q in range(NZL):
         pltpu.make_async_remote_copy(
             src_ref=mem.at[:, :, pl.ds(pl.multiple_of((q * 2 + 1 - core) * OC, OC), OC)],
             dst_ref=pm.at[q], send_sem=pm_send.at[q], recv_sem=pm_recv.at[q],
             device_id=partner, device_id_type=MESH,
         ).start()
-    arrived = r2.at[pl.ds(0, NX * NZ - 1)]
-    pltpu.make_async_copy(arrived, arrived, w_recv).wait()
-
-    for j in range(NY // 2):
-        for v in range(NX * NZ // 2):
-            lo, hi = halves(r2[2 * v, j], r2[2 * v + 1, j])
-            blk[2 * j * (NX * NZ // 2) + v] = lo
-            blk[(2 * j + 1) * (NX * NZ // 2) + v] = hi
+    def tile_load(n):
+        dd = dom(n // NX, n % NX, z)
+        return pltpu.make_async_copy(
+            tiles_hbm.at[dd // 2, :, pl.ds(pl.multiple_of((dd % 2) * NCO, NCO), NCO), :],
+            tl.at[n],
+            tl_sem,
+        )
+
+    def start_tile(n, _):
+        tile_load(n).start()
+        return 0
+
+    lax.fori_loop(0, NY * NX, start_tile, 0)
+
+    arrived = ra.at[z, pl.ds(0, NY * NX - 1)]
+    pltpu.make_async_copy(arrived, arrived, a_recv.at[z]).wait()
+
+    def along(zz, i):
+        return pltpu.make_async_remote_copy(
+            src_ref=ra.at[z], dst_ref=ra.at[z], send_sem=z_send.at[i], recv_sem=a_recv.at[z],
+            device_id=(dom(y, x, zz), e), device_id_type=MESH,
+        )
+
+    along(NZ - 1 - z // 2, 0).start()
+    pl.when(z == 0)(along(1, 1).start)
+    for i in (1, 2):
+        zz = (z + i) % NZ
+        pltpu.make_async_copy(ra.at[zz], ra.at[zz], a_recv.at[zz]).wait()
+
+    for b in range(NY * NX * NZ // 2):
+        pair = [ra[dd % NZ, dd // NZ].astype(f32) for dd in (2 * b, 2 * b + 1)]
+        blk[b] = jnp.concatenate(halves(*pair), axis=0).astype(bf16)
     pltpu.make_async_copy(tl, tl, tl_sem).wait()
     small[2].wait()
     slot = x * NY + y
     for g in range(0, NY * NX, 8):
-        group = b_peers[g:g + 8]
+        group = peers[g:g + 8]
         for yy, xx in group:
             n = yy * NX + xx
             b = dom(yy, xx, z) // 2
@@ -182,7 +188,7 @@
             s3[n] = jnp.concatenate([smooth[:LG // 2], smooth[LG // 2:]], axis=1).astype(bf16)
         for peer in group:
             yy, xx = peer
-            if peer is not b_peers[-1]:
+            if peer is not peers[-1]:
                 pltpu.make_async_remote_copy(
                     src_ref=s3.at[yy * NX + xx], dst_ref=r3.at[slot], send_sem=b_send, recv_sem=b_recv,
                     device_id=(dom(yy, xx, z), e), device_id_type=MESH,
@@ -244,11 +250,19 @@
         order = [tiles[g // 2 + first * (g % 2)] for g in range(LEV // 8)]
         out_ref[c] = jnp.concatenate(order, axis=0).astype(bf16)
 
-    for ref, count, sem in ((r1, NY - 1, y_send), (r3, NY * NX - 1, b_send)):
-        sent = ref.at[pl.ds(0, count)]
+    for ref, sem in ((r3, a_send), (r3, b_send)):
+        sent = ref.at[pl.ds(0, NY * NX - 1)]
         pltpu.make_async_copy(sent, sent, sem).wait()
-    for zz in range(1, NZ):
-        sent_to(zz)
+    pltpu.make_async_copy(ra.at[0], ra.at[0], z_send.at[0]).wait()
+
+    @pl.when(z == 0)
+    def _():
+        pltpu.make_async_copy(ra.at[0], ra.at[0], z_send.at[1]).wait()
+
+    @pl.when(z != 0)
+    def _():
+        pltpu.make_async_copy(ra.at[0], ra.at[0], d_send).wait()
+
     for q in range(NZL):
         pltpu.make_async_copy(pm.at[q], pm.at[q], pm_send.at[q]).wait()
     pltpu.make_async_copy(pr3, pr3, p_send).wait()
@@ -274,10 +288,8 @@
             pltpu.VMEM((2, LEV, COLS), bf16),
             pltpu.VMEM((NY * NX, NNZ, NCO, TILE), bf16),
             pltpu.VMEM((NCO, COLS), bf16),
-            pltpu.VMEM((NY, 2, LG, 128), bf16),
-            pltpu.VMEM((NY, 2, LG, 128), bf16),
-            pltpu.VMEM((NX, NY // 2, LG, 128), bf16),
-            pltpu.VMEM((NX * NZ, NY // 2, LG, 128), bf16),
+            pltpu.VMEM((NY * NX, LG // 2, 128), bf16),
+            pltpu.VMEM((NZ, NY * NX, LG // 2, 128), bf16),
             pltpu.VMEM((NY * NX * NZ // 2, LG, 128), bf16),
             pltpu.VMEM((NY * NX, LG // 2, 128), bf16),
             pltpu.VMEM((NY * NX, LG // 2, 128), bf16),
@@ -286,7 +298,7 @@
             pltpu.VMEM((NZL - 1, 2 * LEV, OC), bf16),
             pltpu.VMEM((NZL, 2 * LEV, OC), bf16),
             dma((3,)), dma((COLS // CH, 2)), dma,
-            dma, dma, dma((NZ,)), dma, dma, dma,
+            dma, dma, dma((NZ,)), dma((2,)), dma, dma,
             dma((NZL,)), dma((NZL,)), dma, dma, dma((NZL - 1,)), dma((NZL,)),
             pltpu.SemaphoreType.REGULAR,
         ],

time: 51.1 us -> 49.1 us (0.961)
  the two profiles are of different devices: /device:TPU:1 before, /device:TPU:64 now
where the time goes in v5:
time: 49.1 us; the launch traced here: 48.9 us
  Pallas kernels  47.4 us (97%)
  local copies, waits for them, and re-layouts  1.56 us (3%)
    pallas_call x1, Pallas kernels, shards(): pl.pallas_call(kernel, name='covary', out_shape=jax.ShapeDtypeStruct((2,...  47.4 us
    unnamed x1, local copies, waits for them, and re-layouts  1.56 us

profile of v5, /device:TPU:64, one launch (start us, length us, event | category | flops | bytes accessed | tf_op | source)
XLA Modules:
  0.0 48.9 jit_solution(16125682845455528590)
XLA Ops:
  0.0 47.4 %covary.1 = bf16[2,120,256]{2,1,0:T(8,128)(2,1)} custom-call(bf16[4,120,2048]{2,1,0:T(8,128)(2,1)} %bitcast.3, bf16[2,120,2048]{2,1,0:T(8,128)(2,1)} %inc_hbm.1, f32[120,120]{1,0:T(8,128)} %vert_hbm.1, bf16[48,4,128,128]{3,2,1,0:T(8,128)(2,1)} %tiles_hbm.1, s32[4,48]{1,0:T(4,128)} %bitcast.5, s32[1,2048]{1,0:T(1,128)} %bitcast.4), custom_call_target="tpu_custom_call" | custom-call | tf_op jit(solution)/shard_map/covary/pallas_call | solution.py:277
  47.4 1.6 %copy.8 = bf16[2,120,256]{2,1,0:T(8,128)(2,1)} copy(bf16[2,120,256]{2,1,0:T(8,128)(2,1)} %covary.1) | data formatting | bytes 245760

commit v6 on v5

--- a/solution.py
+++ b/solution.py
@@ -211,12 +211,12 @@
     def packed(ref, s):
         return ref[s * NY:(s + 1) * NY].astype(f32).reshape(NY * LG // 2, 128).astype(bf16)
 
-    local = [packed(r3, s) for s in range(4)] + [packed(pr3, s) for s in range(4)]
+    local = jnp.concatenate([packed(ref, s) for ref in (r3, pr3) for s in range(4)], axis=0)
     none = jnp.zeros((NCO, OC), bf16)
 
-    def term(s, field, hot):
-        back = [jnp.dot(local[s], h, preferred_element_type=f32) for h in hot]
-        return rows(field.astype(f32)) * jnp.concatenate(back, axis=0)[:LEV]
+    def term(s, field, back):
+        at = slice(s * NY * LG // 2, (s + 1) * NY * LG // 2)
+        return rows(field.astype(f32)) * jnp.concatenate([b[at] for b in back], axis=0)[:LEV]
 
     far = zl // 2
     targets = [3 * (1 - far), 2 - far, zl + 1 - 2 * (zl % 2), zl]
@@ -225,9 +225,10 @@
         at = pl.ds(pl.multiple_of((q * 2 + core) * OC, OC), OC)
         hot = onehot[:, at]
         hot = jnp.concatenate([hot, none], axis=0), jnp.concatenate([none, hot], axis=0)
+        back = [jnp.dot(local, h, preferred_element_type=f32) for h in hot]
         parts = [
-            sum(term(k * 2 + c, mem[k * 2 + c, :, at], hot) for k in range(2))
-            + sum(term(4 + k * 2 + c, pm[q, k * 2 + c], hot) for k in range(2))
+            sum(term(k * 2 + c, mem[k * 2 + c, :, at], back) for k in range(2))
+            + sum(term(4 + k * 2 + c, pm[q, k * 2 + c], back) for k in range(2))
             for c in range(2)
         ]
         both = jnp.concatenate(parts, axis=0)

time: 49.1 us -> 49.1 us (level)
  no operation moved by 1% of the time
where the time goes in v6:
time: 49.1 us; the launch traced here: 48.9 us
  Pallas kernels  47.4 us (97%)
  local copies, waits for them, and re-layouts  1.56 us (3%)
    pallas_call x1, Pallas kernels, shards(): pl.pallas_call(kernel, name='covary', out_shape=jax.ShapeDtypeStruct((2,...  47.4 us
    unnamed x1, local copies, waits for them, and re-layouts  1.56 us

profile of v6, /device:TPU:64, one launch (start us, length us, event | category | flops | bytes accessed | tf_op | source)
XLA Modules:
  0.0 48.9 jit_solution(10912858129095973487)
XLA Ops:
  0.0 47.4 %covary.1 = bf16[2,120,256]{2,1,0:T(8,128)(2,1)} custom-call(bf16[4,120,2048]{2,1,0:T(8,128)(2,1)} %bitcast.3, bf16[2,120,2048]{2,1,0:T(8,128)(2,1)} %inc_hbm.1, f32[120,120]{1,0:T(8,128)} %vert_hbm.1, bf16[48,4,128,128]{3,2,1,0:T(8,128)(2,1)} %tiles_hbm.1, s32[4,48]{1,0:T(4,128)} %bitcast.5, s32[1,2048]{1,0:T(1,128)} %bitcast.4), custom_call_target="tpu_custom_call" | custom-call | tf_op jit(solution)/shard_map/covary/pallas_call | solution.py:278
  47.4 1.6 %copy.8 = bf16[2,120,256]{2,1,0:T(8,128)(2,1)} copy(bf16[2,120,256]{2,1,0:T(8,128)(2,1)} %covary.1) | data formatting | bytes 245760
